TPU v7x, 256 devices: a whole 4x4x8 slice. The times are simulated.
256 devices in a mesh: head: 8 (over y, x_lo), tok: 32 (over x_hi, z, core).
Axes of the slice: x: 4 (x_hi: 2, x_lo: 2; x = x_hi * 2 + x_lo), y: 4, z: 8, core: 2. Of those that a mesh axis runs over, the one named last changes fastest.
Arguments:
- head_outputs: bfloat16 [1024, 8192], P('tok', 'head'), may hold values from -6 to 6
- dec_bias: float32 [8192], P('head'), may hold values from -3 to 3
- enc_bias: float32 [65536], P('tok'), may hold values from -3 to 3
- enc_weight: bfloat16 [8192, 65536], P('head', 'tok'), may hold values from -0.0625 to 0.0625
- dec_weight: bfloat16 [65536, 8192], P('tok', 'head'), may hold values from -0.75 to 0.75
- out_weight: bfloat16 [8192, 8192], P('head', 'tok'), may hold values from -0.0625 to 0.0625
- active_ids: int32 [1024, 128], replicated, may hold values from 0 to 65535, as said below
Outputs:
- reconstruction: bfloat16 [1024, 8192], P('tok', 'head')
- projected: bfloat16 [1024, 8192], P('tok', 'head')
Inputs may be any that keep to these rules, and one draw needn't show every extreme that they name: `active_ids`: entry j of each row lies among the latents j * 512 to (j + 1) * 512 - 1, so the 128 entries of a row are different.
All inputs are finite; a program needn't handle non-finite values.
Results may differ from a plain program's by a relative error of at most 0.0061.
Values may be sent and summed in bfloat16 or wider, within the bound.
A program may use at most 128 MiB of HBM per device.

v0:
```python
import jax
import jax.numpy as jnp
from jax import lax
from jax.sharding import PartitionSpec as P


def latent_mask(id_rows, lat_start, lat_count):
    row_count = id_rows.shape[0]
    shifted = id_rows - lat_start
    inside = (shifted >= 0) & (shifted < lat_count)
    shifted = jnp.where(inside, shifted, lat_count)
    row_ids = jnp.arange(row_count, dtype=jnp.int32)[:, None]
    return jnp.zeros((row_count, lat_count), jnp.float32).at[row_ids, shifted].set(1.0, mode="drop")


def dense_decoder(latents, dec_weight):

    def decode(start, count):
        return jnp.dot(latents, dec_weight, preferred_element_type=jnp.float32)

    return decode


def on_device(head_outputs, dec_bias, enc_bias, enc_weight, dec_weight, out_weight, active_ids):
    centered = (head_outputs.astype(jnp.float32) - dec_bias[None, :]).astype(jnp.bfloat16)
    lat_count = enc_weight.shape[1]
    lat_start = lax.axis_index("tok") * lat_count
    partial_pre = jnp.dot(
        lax.all_gather(centered, "tok", axis=0, tiled=True),
        enc_weight,
        preferred_element_type=jnp.float32,
    )
    pre = lax.psum(partial_pre, "head") + enc_bias[None, :]
    mask = latent_mask(active_ids, lat_start, lat_count)
    latents = (mask * jnp.maximum(pre, 0.0)).astype(jnp.bfloat16)
    decode = dense_decoder(latents, dec_weight)
    decoded = lax.psum_scatter(
        decode(jnp.int32(0), head_outputs.shape[0] * lax.axis_size("tok")),
        "tok",
        scatter_dimension=0,
        tiled=True,
    )
    reconstruction = (decoded + dec_bias[None, :]).astype(jnp.bfloat16)
    partial_out = jnp.dot(
        reconstruction,
        lax.all_gather(out_weight, "tok", axis=1, tiled=True),
        preferred_element_type=jnp.float32,
    )
    projected = lax.psum_scatter(partial_out, "head", scatter_dimension=1, tiled=True).astype(
        jnp.bfloat16
    )
    return (reconstruction, projected)


def solution(mesh):
    return jax.shard_map(
        on_device,
        mesh=mesh,
        in_specs=(
            P("tok", "head"),
            P("head"),
            P("tok"),
            P("head", "tok"),
            P("tok", "head"),
            P("head", "tok"),
            P(),
        ),
        out_specs=(P("tok", "head"), P("tok", "head")),
        check_vma=False,
    )
```

profile of v0, /device:TPU:4, one launch (start us, length us, event | category | flops | bytes accessed | tf_op | source)
XLA Modules:
  0.0 947.2 jit_solution(17735549942467260121)
XLA Ops:
  7.2 0.0 all-gather.3.cloned.1.call-start
  7.2 1.5 subtract_convert_fusion
  8.7 0.0 all-reduce.2.cloned.1.call-start
  8.8 83.0 %all-gather.3.cloned.1.call-done = bf16[1024,1024]{1,0:T(8,128)(2,1)} async-done(((bf16[32,1024]{1,0:T(8,128)(2,1)}), bf16[1024,1024]{1,0:T(8,128)(2,1)}) %all-gather.3.cloned.1.call-update) | async-done | bytes 2097168 | tf_op jit(solution)/shard_map/all_gather | solution.py:29
  91.8 10.5 %fusion.7 = f32[1024,2048]{1,0:T(8,128)} fusion(bf16[1024,1024]{1,0:T(8,128)(2,1)} %all-gather.3.cloned.1.call-done, bf16[1024,2048]{1,0:T(8,128)(2,1)} %param.10), kind=kOutput, calls=%fused_computation.16 | convolution fusion | flops 4294967296 | bytes 14680064 | tf_op jit(solution)/shard_map/dot_general | solution.py:28
  102.4 0.0 reduce-scatter.3.cloned.1.call-start
  102.4 1.0 copy-done
  103.4 0.1 fusion.5
  103.6 0.1 multiply_reduce_fusion
  103.7 0.3 and_reduce_fusion
  104.0 0.1 select_bitcast_fusion
  104.1 482.1 %scatter_custom_fusion = f32[2097152]{0:T(1024)} fusion(s32[131072]{0:T(1024)S(1)} %select_bitcast_fusion, f32[131072]{0:T(1024)S(1)} %broadcast.26, f32[]{:T(128)} %constant.5.clone.1), kind=kCustom, calls=%fused_computation.3 | custom fusion | bytes 8388612
  586.2 9.3 reshape.11
  595.5 13.4 %fusion = f32[1024,1024]{1,0:T(8,128)} fusion(bf16[2048,1024]{1,0:T(8,128)(2,1)} %param.11, f32[1024,2048]{1,0:T(8,128)} %reshape.11, f32[1024,2048]{1,0:T(8,128)} %all-reduce.2.cloned.1.call-done, f32[2048]{0:T(1024)S(1)} %copy-done.5), kind=kOutput, calls=%fused_computation.2 | convolution fusion | flops 4303355904 | bytes 25174016 | tf_op jit(solution)/shard_map/dot_general | solution.py:19
  608.9 0.0 all-gather.5.cloned.1.call-start
  608.9 0.5 all-gather.5.cloned.1.call-update
  609.5 0.2 reduce-scatter.5.cloned.1.call-start
  609.7 125.0 %reduce-scatter.3.cloned.1.call-done = f32[32,1024]{1,0:T(8,128)} async-done(((f32[1024,1024]{1,0:T(8,128)}), f32[32,1024]{1,0:T(8,128)}) %reduce-scatter.3.cloned.1.call-update) | async-done | bytes 131088 | tf_op jit(solution)/shard_map/reduce_scatter | solution.py:37
  734.7 0.9 add_convert_fusion
  735.7 152.1 %all-gather.5.cloned.1.call-done = bf16[1024,8192]{1,0:T(8,128)(2,1)} async-done(((bf16[1024,256]{1,0:T(8,128)(2,1)}), bf16[1024,8192]{1,0:T(8,128)(2,1)}) %all-gather.5.cloned.1.call-update) | async-done | bytes 16777232 | tf_op jit(solution)/shard_map/all_gather | solution.py:46
  887.8 9.7 %fusion.8 = f32[32,8192]{1,0:T(8,128)} fusion(bf16[32,1024]{1,0:T(8,128)(2,1)S(1)} %add_convert_fusion, bf16[1024,8192]{1,0:T(8,128)(2,1)} %all-gather.5.cloned.1.call-done), kind=kOutput, calls=%fused_computation.17 | convolution fusion | flops 536870912 | bytes 17891328 | tf_op jit(solution)/shard_map/dot_general | solution.py:44
  897.5 0.0 reduce-scatter.5.cloned.1.call-update
  897.5 41.6 %reduce-scatter.5.cloned.1.call-done = f32[32,1024]{1,0:T(8,128)} async-done(((f32[32,8192]{1,0:T(8,128)}), f32[32,1024]{1,0:T(8,128)}) %reduce-scatter.5.cloned.1.call-update) | async-done | bytes 131088 | tf_op jit(solution)/shard_map/reduce_scatter | solution.py:49
  939.1 1.5 convert_element_type.19
  (17 shorter events, 0.1 us)
Async XLA Ops:
  7.2 84.6 %all-gather.3.cloned.1.call-start = ((), (), s32[]{:S(2)}) async-start(), calls=%async_computation.2 | async-start | bytes 2162688 | tf_op jit(solution)/shard_map/all_gather | solution.py:29
  8.7 586.7 %all-reduce.2.cloned.1.call-start = ((), (), s32[]{:S(2)}) async-start(), calls=%async_computation.3 | async-start | bytes 16777216 | tf_op jit(solution)/shard_map/psum | solution.py:33
  102.3 1.0 copy-start
  102.3 1.2 copy-start.4
  102.3 1.4 copy-start.3
  102.4 632.4 %reduce-scatter.3.cloned.1.call-start = ((), (), s32[]{:S(2)}) async-start(), calls=%async_computation.4 | async-start | bytes 4325376 | tf_op jit(solution)/shard_map/reduce_scatter | solution.py:37
  586.2 9.3 copy-start.5
  595.5 139.3 %copy-start.2 = (f32[1024]{0:T(1024)S(1)}, f32[1024]{0:T(1024)}, u32[]{:S(2)}) copy-start(f32[1024]{0:T(1024)} %param.8) | copy-start | bytes 12292
  608.9 278.9 %all-gather.5.cloned.1.call-start = ((), (), s32[]{:S(2)}) async-start(), calls=%async_computation.5 | async-start | bytes 17301504 | tf_op jit(solution)/shard_map/all_gather | solution.py:46
  609.5 329.7 %reduce-scatter.5.cloned.1.call-start = ((), (), s32[]{:S(2)}) async-start(), calls=%async_computation.6 | async-start | bytes 1179648 | tf_op jit(solution)/shard_map/reduce_scatter | solution.py:49
  735.7 161.9 %copy-start.1 = (bf16[32,1024]{1,0:T(8,128)(2,1)}, bf16[32,1024]{1,0:T(8,128)(2,1)S(1)}, u32[]{:S(2)}) copy-start(bf16[32,1024]{1,0:T(8,128)(2,1)S(1)} %add_convert_fusion) | copy-start | bytes 196612
Sparse Core Ops, SparseCore 0:
  11.3 80.4 all-gather.2
  102.5 343.3 all-reduce.1
  609.0 125.6 reduce-scatter.2
  737.5 150.2 all-gather.4
  897.7 41.4 reduce-scatter.4
where the time goes:
time: 948 us; the launch traced here: 947 us
  local copies, waits for them, and re-layouts  492 us (52%)
  waiting for transfers between devices  402 us (42%)
  matrix products  33.7 us (4%)
  between operations  13.8 us (1%)
    unnamed x14, local copies, waits for them, and re-layouts  483 us
    all_gather x1, waiting for transfers between devices, on_device(): lax.all_gather(out_weight, 'tok', axis=1, tiled=True)  152 us
    reduce_scatter x1, waiting for transfers between devices, on_device(): lax.psum_scatter(decode(jnp.int32(0), head_outputs.shape[0] * lax.axis_si...  125 us
    all_gather x1, waiting for transfers between devices, on_device(): lax.all_gather(centered, 'tok', axis=0, tiled=True)  83 us
    reduce_scatter x1, waiting for transfers between devices, on_device(): lax.psum_scatter(partial_out, 'head', scatter_dimension=1, tiled=True)  41.6 us
  transfers between devices with their start and end apart: 5, of which 4 were waited for; matrix products, arithmetic and copies ran while one was open for 52% of the time, Pallas kernels for 0%

commit v1 on v0

--- a/solution.py
+++ b/solution.py
@@ -2,6 +2,7 @@
 import jax.numpy as jnp
 from jax import lax
 from jax.sharding import PartitionSpec as P
+from jax.lax import all_to_all, axis_size
 
 
 def latent_mask(id_rows, lat_start, lat_count):
@@ -41,10 +42,14 @@
         tiled=True,
     )
     reconstruction = (decoded + dec_bias[None, :]).astype(jnp.bfloat16)
+
+    def find_words(z):
+        return jnp.concatenate(
+            all_to_all(jnp.stack([z] * axis_size("tok"), axis=0), "tok", 0, 0), axis=1
+        )
+
     partial_out = jnp.dot(
-        reconstruction,
-        lax.all_gather(out_weight, "tok", axis=1, tiled=True),
-        preferred_element_type=jnp.float32,
+        reconstruction, find_words(out_weight), preferred_element_type=jnp.float32
     )
     projected = lax.psum_scatter(partial_out, "head", scatter_dimension=1, tiled=True).astype(
         jnp.bfloat16

time: 948 us -> 868 us (0.916)
  waiting for transfers between devices: 402 us -> 303 us
  starting transfers between devices: 0.38 us -> 12.1 us
    all_gather x1 -> x0, waiting for transfers between devices: 152 us -> none  [on_device(): lax.all_gather(out_weight, 'tok', axis=1, tiled=True)]
    all_gather x1, waiting for transfers between devices: 83 us -> 132 us  [on_device(): lax.all_gather(centered, 'tok', axis=0, tiled=True)]
    all_to_all x0 -> x1, starting transfers between devices: none -> 11.8 us  [find_words(): all_to_all(jnp.stack([z] * axis_size('tok'), axis=0), 'tok', 0, 0)]
    unnamed x14 -> x17, local copies, waits for them, and re-layouts: 483 us -> 484 us
  transfers between devices with their start and end apart: 5 -> 5, of which waited for: 4 -> 3; matrix products, arithmetic and copies ran while one was open for 52% -> 60% of each run, Pallas kernels for 0% -> 0%
where the time goes in v1:
time: 868 us; the launch traced here: 867 us
  local copies, waits for them, and re-layouts  500 us (58%)
  waiting for transfers between devices  303 us (35%)
  matrix products  35.7 us (4%)
  between operations  13.9 us (2%)
  starting transfers between devices  12.1 us (1%)
    unnamed x17, local copies, waits for them, and re-layouts  484 us
    all_gather x1, waiting for transfers between devices, on_device(): lax.all_gather(centered, 'tok', axis=0, tiled=True)  132 us
    reduce_scatter x1, waiting for transfers between devices, on_device(): lax.psum_scatter(decode(jnp.int32(0), head_outputs.shape[0] * lax.axis_si...  128 us
    reduce_scatter x1, waiting for transfers between devices, on_device(): lax.psum_scatter(partial_out, 'head', scatter_dimension=1, tiled=True)  42.9 us
  transfers between devices with their start and end apart: 5, of which 3 were waited for; matrix products, arithmetic and copies ran while one was open for 60% of the time, Pallas kernels for 0%

profile of v1, /device:TPU:4, one launch (start us, length us, event | category | flops | bytes accessed | tf_op | source)
XLA Modules:
  0.0 867.5 jit_solution(17155444715181003260)
XLA Ops:
  7.2 1.2 copy.9
  8.4 6.0 stack.2
  14.4 11.8 %all-to-all-start = ((bf16[32,1024,256]{1,2,0:T(8,128)(2,1)}), bf16[32,1024,256]{1,2,0:T(8,128)(2,1)}, u32[]{:S(2)}, u32[]{:S(2)}) async-start(bf16[32,1024,256]{1,2,0:T(8,128)(2,1)} %stack.2), calls=%async_computation.1 | async-start | bytes 33554432 | tf_op jit(solution)/shard_map/all_to_all | solution.py:48
  26.2 0.0 all-gather.2.cloned.1.call-start
  26.3 0.6 subtract_convert_fusion
  26.9 0.0 all-reduce.2.cloned.1.call-start
  27.0 132.0 %all-gather.2.cloned.1.call-done = bf16[1024,1024]{1,0:T(8,128)(2,1)} async-done(((bf16[32,1024]{1,0:T(8,128)(2,1)}), bf16[1024,1024]{1,0:T(8,128)(2,1)}) %all-gather.2.cloned.1.call-update) | async-done | bytes 2097168 | tf_op jit(solution)/shard_map/all_gather | solution.py:30
  159.0 10.5 %fusion.7 = f32[1024,2048]{1,0:T(8,128)} fusion(bf16[1024,1024]{1,0:T(8,128)(2,1)} %all-gather.2.cloned.1.call-done, bf16[1024,2048]{1,0:T(8,128)(2,1)} %param.10), kind=kOutput, calls=%fused_computation.16 | convolution fusion | flops 4294967296 | bytes 14680064 | tf_op jit(solution)/shard_map/dot_general | solution.py:29
  169.5 0.0 reduce-scatter.3.cloned.1.call-start
  169.6 1.0 copy-done
  170.6 0.1 fusion.5
  170.7 0.1 multiply_reduce_fusion
  170.9 0.3 and_reduce_fusion
  171.2 0.1 select_bitcast_fusion
  171.3 482.1 %scatter_custom_fusion = f32[2097152]{0:T(1024)} fusion(s32[131072]{0:T(1024)S(1)} %select_bitcast_fusion, f32[131072]{0:T(1024)S(1)} %broadcast.28, f32[]{:T(128)} %constant.5.clone.1), kind=kCustom, calls=%fused_computation.3 | custom fusion | bytes 8388612
  653.4 9.2 %reshape.21 = f32[1024,2048]{1,0:T(8,128)} reshape(f32[2097152]{0:T(1024)} %scatter_custom_fusion) | data formatting | bytes 16777216 | tf_op jit(solution)/shard_map/scatter | solution.py:14
  662.6 13.4 %fusion = f32[1024,1024]{1,0:T(8,128)} fusion(bf16[2048,1024]{1,0:T(8,128)(2,1)} %param.11, f32[1024,2048]{1,0:T(8,128)} %reshape.21, f32[1024,2048]{1,0:T(8,128)} %all-reduce.2.cloned.1.call-done, f32[2048]{0:T(1024)S(1)} %copy-done.6), kind=kOutput, calls=%fused_computation.2 | convolution fusion | flops 4303355904 | bytes 25174016 | tf_op jit(solution)/shard_map/dot_general | solution.py:20
  676.0 0.2 reduce-scatter.5.cloned.1.call-start
  676.2 127.6 %reduce-scatter.3.cloned.1.call-done = f32[32,1024]{1,0:T(8,128)} async-done(((f32[1024,1024]{1,0:T(8,128)}), f32[32,1024]{1,0:T(8,128)}) %reduce-scatter.3.cloned.1.call-update) | async-done | bytes 131088 | tf_op jit(solution)/shard_map/reduce_scatter | solution.py:38
  803.8 0.9 add_convert_fusion
  804.7 11.8 %fusion.8 = f32[32,8192]{1,0:T(8,128)} fusion(bf16[32,1024]{1,0:T(8,128)(2,1)S(1)} %add_convert_fusion, bf16[1024,8192]{0,1:T(8,128)(2,1)} %bitcast.3), kind=kOutput, calls=%fused_computation.17 | convolution fusion | flops 536870912 | bytes 17891328 | tf_op jit(solution)/shard_map/dot_general | solution.py:51
  816.5 0.0 reduce-scatter.5.cloned.1.call-update
  816.5 42.9 %reduce-scatter.5.cloned.1.call-done = f32[32,1024]{1,0:T(8,128)} async-done(((f32[32,8192]{1,0:T(8,128)}), f32[32,1024]{1,0:T(8,128)}) %reduce-scatter.5.cloned.1.call-update) | async-done | bytes 131088 | tf_op jit(solution)/shard_map/reduce_scatter | solution.py:54
  859.4 1.5 convert_element_type.19
  (20 shorter events, 0.2 us)
Async XLA Ops:
  14.4 11.8 %copy-start.2 = (bf16[32,1024]{1,0:T(8,128)(2,1)S(1)}, bf16[32,1024]{1,0:T(8,128)(2,1)}, u32[]{:S(2)}) copy-start(bf16[32,1024]{1,0:T(8,128)(2,1)} %param.7) | copy-start | bytes 196612
  14.4 11.9 %copy-start.3 = (f32[1024]{0:T(1024)S(1)}, f32[1024]{0:T(1024)}, u32[]{:S(2)}) copy-start(f32[1024]{0:T(1024)} %param.8) | copy-start | bytes 12292
  14.4 790.3 %all-to-all-start = ((bf16[32,1024,256]{1,2,0:T(8,128)(2,1)}), bf16[32,1024,256]{1,2,0:T(8,128)(2,1)}, u32[]{:S(2)}, u32[]{:S(2)}) async-start(bf16[32,1024,256]{1,2,0:T(8,128)(2,1)} %stack.2), calls=%async_computation.1 | async-start | bytes 33554432 | tf_op jit(solution)/shard_map/all_to_all | solution.py:48
  26.2 132.8 %all-gather.2.cloned.1.call-start = ((), (), s32[]{:S(2)}) async-start(), calls=%async_computation.3 | async-start | bytes 2162688 | tf_op jit(solution)/shard_map/all_gather | solution.py:30
  26.9 635.7 %all-reduce.2.cloned.1.call-start = ((), (), s32[]{:S(2)}) async-start(), calls=%async_computation.4 | async-start | bytes 16777216 | tf_op jit(solution)/shard_map/psum | solution.py:34
  169.5 1.0 copy-start
  169.5 1.2 copy-start.5
  169.5 1.4 copy-start.4
  169.5 634.3 %reduce-scatter.3.cloned.1.call-start = ((), (), s32[]{:S(2)}) async-start(), calls=%async_computation.5 | async-start | bytes 4325376 | tf_op jit(solution)/shard_map/reduce_scatter | solution.py:38
  653.3 9.3 %copy-start.6 = (f32[2048]{0:T(1024)S(1)}, f32[2048]{0:T(1024)}, u32[]{:S(2)}) copy-start(f32[2048]{0:T(1024)} %param.9) | copy-start | bytes 24580
  676.0 183.4 %reduce-scatter.5.cloned.1.call-start = ((), (), s32[]{:S(2)}) async-start(), calls=%async_computation.6 | async-start | bytes 1179648 | tf_op jit(solution)/shard_map/reduce_scatter | solution.py:54
  804.7 11.8 %copy-start.1 = (bf16[32,1024]{1,0:T(8,128)(2,1)}, bf16[32,1024]{1,0:T(8,128)(2,1)S(1)}, u32[]{:S(2)}) copy-start(bf16[32,1024]{1,0:T(8,128)(2,1)S(1)} %add_convert_fusion) | copy-start | bytes 196612
Sparse Core Ops, SparseCore 0:
  30.4 128.5 all-gather.1
  169.7 444.9 all-reduce.1
  676.1 127.6 reduce-scatter.2
  816.7 42.7 reduce-scatter.4
